TPU v7x, 256 devices: a whole 4x4x8 slice. The times are simulated.
256 devices in a mesh: pitch: 4 (over y), span: 4 (over x_hi, core), axial: 16 (over x_lo, z).
Axes of the slice: x: 4 (x_hi: 2, x_lo: 2; x = x_hi * 2 + x_lo), y: 4, z: 8, core: 2. Of those that a mesh axis runs over, the one named last changes fastest.
Arguments:
- state: float32 [5, 9, 16, 32, 2048], P(None, None, 'pitch', 'span', 'axial'), may hold values from -2 to 2
- source: float32 [5, 9, 16, 32, 2048], P(None, None, 'pitch', 'span', 'axial'), may hold values from -6 to 6
- velocity: float32 [3, 16, 32, 2048], P(None, 'pitch', 'span', 'axial'), may hold values from -4 to 4
- coupling: float32 [5, 5], replicated, may hold values from -2.5 to 2.5
- rotor: float32 [2], replicated, may hold values from 0.5 to 2.5
- face_map: int32 [32, 2048], P('span', 'axial'), may hold values from 0 to 1023, as said below
Outputs:
- smoothed: float32 [5, 9, 16, 32, 2048], P(None, None, 'pitch', 'span', 'axial')
Inputs may be any that keep to these rules, and one draw needn't show every extreme that they name: `face_map`: within each aligned block of 8 hub-to-tip by 128 streamwise cells, the entries are a permutation of 0 to 1023.
All inputs are finite; a program needn't handle non-finite values.
Results may differ from a plain program's by a relative error of at most 0.0001.
Values sent between devices are 32-bit elements; how exact they have to be, the bound alone decides.
A program may use at most 128 MiB of HBM per device.

v0:
```python
import functools
import math

import jax
import jax.numpy as jnp
from jax import lax
from jax.experimental import pallas as pl
from jax.experimental.pallas import tpu as pltpu
from jax.sharding import PartitionSpec as P

NVAR = 5
NT = 9
PC = 4
CS = 8
CA = 128
ROWS = PC * CS
CELLS = (PC, CS, CA)
SWEEPS = 3
ROUNDS = SWEEPS + 1
VISCOSITY = 0.1
CFL_RATIO = 3.0
MESH = pl.DeviceIdType.MESH
HALF = (NT - 1) // 2


def roll(values, shift, axis):
    shift %= values.shape[axis]
    return values if shift == 0 else pltpu.roll(values, shift, axis)


def cells(rows):
    return rows.reshape(CELLS)


def flat(values):
    return values.reshape(ROWS, CA)


def kernel(
    state_ref, source_ref, velocity_ref, coupling_ref, rotor_ref, map_ref,
    out_ref,
    field, base, forcing, velocity, result, coef, weight, table, pick,
    pitch_ghost, span_send, span_ghost, axial_send, axial_ghost,
    load_sem, store_sem, send_sem, recv_sem,
):
    place = {a: lax.axis_index(a) for a in ("pitch", "span", "axial")}
    count = {a: lax.axis_size(a) for a in ("pitch", "span", "axial")}
    has_lower = {a: place[a] > 0 for a in ("span", "axial")}
    has_upper = {a: place[a] < count[a] - 1 for a in ("span", "axial")}
    pitch_up = lax.rem(place["pitch"] + 1, count["pitch"])
    pitch_down = lax.rem(place["pitch"] + count["pitch"] - 1, count["pitch"])
    on_first = place["pitch"] == 0
    on_last = place["pitch"] == count["pitch"] - 1

    barrier = pltpu.get_barrier_semaphore()
    for target in (pitch_up, pitch_down):
        pl.semaphore_signal(barrier, inc=1, device_id={"pitch": target}, device_id_type=MESH)
    for axis in ("span", "axial"):
        for there, step in ((has_lower[axis], -1), (has_upper[axis], 1)):

            @pl.when(there)
            def _():
                pl.semaphore_signal(
                    barrier, inc=1, device_id={axis: place[axis] + step}, device_id_type=MESH
                )

    loads = [
        pltpu.make_async_copy(state_ref, field.at[0], load_sem.at[0]),
        pltpu.make_async_copy(velocity_ref, velocity, load_sem.at[1]),
        pltpu.make_async_copy(source_ref, forcing, load_sem.at[2]),
    ]
    for load in loads:
        load.start()

    lane = lax.broadcasted_iota(jnp.int32, (PC, CS, CA), 2)
    row = lax.broadcasted_iota(jnp.int32, (CS, CA), 0)
    lane2 = lax.broadcasted_iota(jnp.int32, (CS, CA), 1)
    row4 = lax.broadcasted_iota(jnp.int32, (PC, CS, CA), 1)

    def transfers(k, v):
        source_of = state_ref if k == 0 else field.at[k]
        plan = (
            (None, None, source_of.at[v, :, pl.ds(ROWS - CS, CS)], pitch_ghost.at[k, 0, v], "pitch", pitch_up),
            (None, None, source_of.at[v, :, pl.ds(0, CS)], pitch_ghost.at[k, 1, v], "pitch", pitch_down),
            (has_upper["span"], has_lower["span"], span_send.at[k, 0, v], span_ghost.at[k, 0, v], "span", place["span"] + 1),
            (has_lower["span"], has_upper["span"], span_send.at[k, 1, v], span_ghost.at[k, 1, v], "span", place["span"] - 1),
            (has_upper["axial"], has_lower["axial"], axial_send.at[k, 0, v], axial_ghost.at[k, 0, v], "axial", place["axial"] + 1),
            (has_lower["axial"], has_upper["axial"], axial_send.at[k, 1, v], axial_ghost.at[k, 1, v], "axial", place["axial"] - 1),
        )
        for d, (sends, receives, src, dst, axis, target) in enumerate(plan):
            copy = pltpu.make_async_remote_copy(
                src_ref=src,
                dst_ref=dst,
                send_sem=send_sem.at[k, v, d],
                recv_sem=recv_sem.at[k, v, d],
                device_id={axis: target},
                device_id_type=MESH,
            )
            yield sends, receives, copy

    def guarded(condition, action):
        if condition is None:
            action()
        else:
            pl.when(condition)(action)

    def start(k, v):
        for sends, _, copy in transfers(k, v):
            guarded(sends, copy.start)

    def await_arrival(k, v):
        for _, receives, copy in transfers(k, v):
            guarded(receives, copy.wait_recv)

    def await_departure(k, v):
        for sends, _, copy in transfers(k, v):
            guarded(sends, copy.wait_send)

    def pack_axial(k, v, first, last):
        for d, packed in ((0, last), (1, first)):
            tile = packed[0]
            for p in range(1, PC):
                tile = jnp.where(lane2 >= 16 * p, roll(packed[p], 16 * p, 1), tile)
            axial_send[k, d, v] = tile

    def pack_span(k, v):
        for i in range(NT):
            at = pl.ds(i * PC, PC)
            span_send[k, 0, v, at, :] = field[k, v, i, pl.ds(CS - 1, PC, CS), :]
            span_send[k, 1, v, at, :] = field[k, v, i, pl.ds(0, PC, CS), :]

    def add_faces(values, i, packs):
        first, last = packs
        return (
            jnp.where(lane == i, roll(values, i, 2), first),
            jnp.where(lane == i, roll(values, i + 1, 2), last),
        )

    empty = jnp.zeros((PC, CS, CA), jnp.float32)

    for d, there in ((0, has_lower), (1, has_upper)):
        for axis, ghost in (("span", span_ghost), ("axial", axial_ghost)):

            @pl.when(jnp.logical_not(there[axis]))
            def _():
                def clear(v, carry):
                    for k in range(ROUNDS):
                        ghost[k, d, v] = jnp.zeros(ghost.shape[3:], jnp.float32)
                    return carry

                lax.fori_loop(0, NVAR, clear, 0)

    loads[0].wait()

    def pack_state(v, carry):
        packs = (empty, empty)
        for i in range(NT):
            packs = add_faces(cells(field[0, v, i]), i, packs)
        pack_axial(0, v, *packs)
        pack_span(0, v)
        return carry

    lax.fori_loop(0, NVAR, pack_state, 0)

    waits = 2 + sum(
        there[a].astype(jnp.int32) for there in (has_lower, has_upper) for a in ("span", "axial")
    )
    pl.semaphore_wait(barrier, waits)

    def send_state(v, carry):
        start(0, v)
        return carry

    lax.fori_loop(0, NVAR, send_state, 0)

    loads[1].wait()
    radius = [jnp.abs(velocity[d]) + 2.0 * VISCOSITY for d in range(3)]
    scale = CFL_RATIO / (radius[0] + radius[1] + radius[2])
    smoothing = []
    for d in range(3):
        ratio = radius[d] * scale
        smoothing.append(0.25 * jnp.maximum(ratio * ratio - 1.0, 0.0))
    inverse_diagonal = 1.0 / (1.0 + 2.0 * (smoothing[0] + smoothing[1] + smoothing[2]))
    centre = jnp.full((PC, CS, CA), -6.0 * VISCOSITY, jnp.float32)
    for d in range(3):
        weight[d] = smoothing[d] * inverse_diagonal
        speed = velocity[d]
        coef[2 * d] = jnp.maximum(speed, 0.0) + VISCOSITY
        coef[2 * d + 1] = VISCOSITY - jnp.minimum(speed, 0.0)
        centre = centre - jnp.abs(speed)
    weight[3] = inverse_diagonal
    coef[6] = centre

    frequency = rotor_ref[0]
    rates = [
        frequency * (0.5 * (1 - 2 * (n % 2)) / math.sin(math.pi * n / NT))
        for n in range(1, HALF + 1)
    ]
    loads[2].wait()

    def local_part(v, carry):
        x = [cells(field[0, v, i]) for i in range(NT)]
        own = coef[6]
        for i in range(NT):
            total = cells(forcing[v, i]) + own * x[i]
            for n in range(1, HALF + 1):
                total = total - rates[n - 1] * (x[(i - n) % NT] - x[(i + n) % NT])
            for w in range(NVAR):
                total = total - coupling_ref[v, w] * cells(field[0, w, i])
            field[1, v, i] = flat(total)
        return carry

    lax.fori_loop(0, NVAR, local_part, 0)

    @pl.when(jnp.logical_or(on_first, on_last))
    def _():
        angle = jnp.full((CS, CA), rotor_ref[1], jnp.float32)
        c1 = jnp.cos(angle)
        s1 = jnp.sin(angle) * jnp.where(on_first, 1.0, -1.0)
        c2, s2 = c1 * c1 - s1 * s1, 2.0 * s1 * c1
        c3, s3 = c2 * c1 - s2 * s1, s2 * c1 + c2 * s1
        c4, s4 = c2 * c2 - s2 * s2, 2.0 * s2 * c2
        for n in range(NT):
            total = jnp.full((CS, CA), 1.0 / NT, jnp.float32)
            for h, (c, s) in enumerate(((c1, s1), (c2, s2), (c3, s3), (c4, s4)), 1):
                theta = h * 2.0 * math.pi * n / NT
                total = total + (2.0 / NT * math.cos(theta)) * c - (2.0 / NT * math.sin(theta)) * s
            table[n] = total
        forward = map_ref[...]
        pick[0] = lax.shift_right_logical(forward, 7)
        pick[1] = lax.bitwise_and(forward, CA - 1)

    @pl.when(on_last)
    def _():
        rows, cols = pick[0], pick[1]
        column = lax.broadcasted_iota(jnp.int32, (CA, CA), 0)
        total = jnp.zeros((2 * CS, CA), jnp.float32)
        for s in range(CS):
            hit = rows[s : s + 1, :] == row
            left = jnp.concatenate(
                [
                    jnp.where(hit, float(s), 0.0),
                    jnp.where(hit, lane2.astype(jnp.float32), 0.0),
                ],
                axis=0,
            )
            right = jnp.where(cols[s : s + 1, :] == column, 1.0, 0.0)
            total = total + lax.dot_general(
                left, right, (((1,), (1,)), ((), ())), preferred_element_type=jnp.float32
            )
        pick[0] = total[:CS].astype(jnp.int32)
        pick[1] = total[CS:].astype(jnp.int32)

    def map_face(k, v):
        slot = jnp.where(on_first, 0, 1)

        @pl.when(jnp.logical_or(on_first, on_last))
        def _():
            rows, cols = pick[0], pick[1]
            picked = []
            for i in range(NT):
                total = jnp.zeros((CS, CA), jnp.float32)
                for s in range(CS):
                    line = pitch_ghost[k, slot, v, i, pl.ds(s, 1), :]
                    taken = jnp.take_along_axis(
                        jnp.broadcast_to(line, (CS, CA)), cols, axis=1, mode="promise_in_bounds"
                    )
                    total = jnp.where(rows == s, taken, total)
                picked.append(total)
            for i in range(NT):
                total = table[0] * picked[i]
                for n in range(1, NT):
                    total = total + table[n] * picked[(i - n) % NT]
                pitch_ghost[k, slot, v, i] = total

    def beside(k, v, i, axial):
        x = cells(field[k, v, i])
        pitch_low = jnp.concatenate([pitch_ghost[k, 0, v, i][None], x[: PC - 1]], axis=0)
        pitch_high = jnp.concatenate([x[1:], pitch_ghost[k, 1, v, i][None]], axis=0)
        lines = [
            jnp.stack(
                [
                    jnp.broadcast_to(span_ghost[k, d, v, pl.ds(i * PC + p, 1), :], (CS, CA))
                    for p in range(PC)
                ]
            )
            for d in range(2)
        ]
        span_low = jnp.where(row4 == 0, lines[0], roll(x, 1, 1))
        span_high = jnp.where(row4 == CS - 1, lines[1], roll(x, -1, 1))
        axial_low = jnp.where(lane == 0, roll(axial[0], -i, 2), roll(x, 1, 2))
        axial_high = jnp.where(lane == CA - 1, roll(axial[1], -i - 1, 2), roll(x, -1, 2))
        return pitch_low, pitch_high, span_low, span_high, axial_low, axial_high

    def unpack_axial(k, v):
        return [
            jnp.stack([roll(axial_ghost[k, d, v], -16 * p, 1) for p in range(PC)])
            for d in range(2)
        ]

    def residual_step(v, carry):
        await_departure(0, v)
        await_arrival(0, v)
        map_face(0, v)
        axial = unpack_axial(0, v)
        packs = (empty, empty)
        for i in range(NT):
            total = cells(field[1, v, i])
            for d, values in enumerate(beside(0, v, i, axial)):
                total = total + coef[d] * values
            field[1, v, i] = flat(total)
            base[v, i] = flat(total * weight[3])
            packs = add_faces(total, i, packs)
        pack_axial(1, v, *packs)
        pack_span(1, v)
        start(1, v)
        return carry

    lax.fori_loop(0, NVAR, residual_step, 0)

    def sweep_step(k, v, carry):
        last = k == ROUNDS - 1
        await_departure(k, v)
        await_arrival(k, v)
        map_face(k, v)
        axial = unpack_axial(k, v)
        packs = (empty, empty)
        for i in range(NT):
            near = beside(k, v, i, axial)
            total = cells(base[v, i])
            for d in range(3):
                total = total + weight[d] * (near[2 * d] + near[2 * d + 1])
            if last:
                result[v, i] = flat(total)
            else:
                field[k + 1, v, i] = flat(total)
                packs = add_faces(total, i, packs)
        if last:
            pltpu.make_async_copy(result.at[v], out_ref.at[v], store_sem.at[v]).start()
        else:
            pack_axial(k + 1, v, *packs)
            pack_span(k + 1, v)
            start(k + 1, v)
        return carry

    for k in range(1, ROUNDS):
        lax.fori_loop(0, NVAR, functools.partial(sweep_step, k), 0)

    def finish(v, carry):
        pltpu.make_async_copy(result.at[v], out_ref.at[v], store_sem.at[v]).wait()
        return carry

    lax.fori_loop(0, NVAR, finish, 0)


def per_device(state, source, velocity, coupling, rotor, face_map):
    block = (NVAR, NT, ROWS, CA)
    anywhere = pl.BlockSpec(memory_space=pl.ANY)
    scalars = pl.BlockSpec(memory_space=pltpu.SMEM)
    f32 = jnp.float32
    out = pl.pallas_call(
        kernel,
        out_shape=jax.ShapeDtypeStruct(block, f32),
        in_specs=[anywhere, anywhere, anywhere, scalars, scalars, pl.BlockSpec(memory_space=pltpu.VMEM)],
        out_specs=anywhere,
        scratch_shapes=[
            pltpu.VMEM((ROUNDS,) + block, f32),
            pltpu.VMEM(block, f32),
            pltpu.VMEM(block, f32),
            pltpu.VMEM((3, PC, CS, CA), f32),
            pltpu.VMEM(block, f32),
            pltpu.VMEM((7, PC, CS, CA), f32),
            pltpu.VMEM((4, PC, CS, CA), f32),
            pltpu.VMEM((NT, CS, CA), f32),
            pltpu.VMEM((2, CS, CA), jnp.int32),
            pltpu.VMEM((ROUNDS, 2, NVAR, NT, CS, CA), f32),
            pltpu.VMEM((ROUNDS, 2, NVAR, NT * PC, CA), f32),
            pltpu.VMEM((ROUNDS, 2, NVAR, NT * PC, CA), f32),
            pltpu.VMEM((ROUNDS, 2, NVAR, CS, CA), f32),
            pltpu.VMEM((ROUNDS, 2, NVAR, CS, CA), f32),
            pltpu.SemaphoreType.DMA((3,)),
            pltpu.SemaphoreType.DMA((NVAR,)),
            pltpu.SemaphoreType.DMA((ROUNDS, NVAR, 6)),
            pltpu.SemaphoreType.DMA((ROUNDS, NVAR, 6)),
        ],
        compiler_params=pltpu.CompilerParams(
            collective_id=0, has_side_effects=True, vmem_limit_bytes=32 * 1024 * 1024
        ),
        cost_estimate=pl.CostEstimate(flops=20_000_000, bytes_accessed=2_300_000, transcendentals=0),
    )(state.reshape(block), source.reshape(block), velocity, coupling, rotor, face_map)
    return out.reshape(state.shape)


def solution(mesh):
    return jax.shard_map(
        per_device,
        mesh=mesh,
        in_specs=(
            P(None, None, "pitch", "span", "axial"),
            P(None, None, "pitch", "span", "axial"),
            P(None, "pitch", "span", "axial"),
            P(),
            P(),
            P("span", "axial"),
        ),
        out_specs=P(None, None, "pitch", "span", "axial"),
        check_vma=False,
    )
```

profile of v0, /device:TPU:3, one launch (start us, length us, event | category | flops | bytes accessed | tf_op | source)
XLA Modules:
  0.0 37.3 jit_solution(3536658905415825923)
XLA Ops:
  0.0 0.0 copy-start.5
  0.0 0.7 %copy-done.5 = f32[2]{0:T(128)S(1)} copy-done((f32[2]{0:T(128)S(1)}, f32[2]{0:T(128)}, u32[]{:S(2)}) %copy-start.5) | copy-done | bytes 32
  0.7 0.0 copy-start
  0.7 1.1 %copy-done = f32[5,9,4,8,128]{4,3,2,1,0:T(8,128)S(1)} copy-done((f32[5,9,4,8,128]{4,3,2,1,0:T(8,128)S(1)}, f32[5,9,4,8,128]{4,3,2,1,0:T(8,128)}, u32[]{:S(2)}) %copy-start) | copy-done | bytes 737304
  1.8 0.0 copy-start.1
  1.8 1.1 %copy-done.1 = f32[5,9,4,8,128]{4,3,2,1,0:T(8,128)S(1)} copy-done((f32[5,9,4,8,128]{4,3,2,1,0:T(8,128)S(1)}, f32[5,9,4,8,128]{4,3,2,1,0:T(8,128)}, u32[]{:S(2)}) %copy-start.1) | copy-done | bytes 737304
  2.9 0.0 copy-start.2
  2.9 0.8 %copy-done.2 = f32[3,4,8,128]{3,2,1,0:T(8,128)S(1)} copy-done((f32[3,4,8,128]{3,2,1,0:T(8,128)S(1)}, f32[3,4,8,128]{3,2,1,0:T(8,128)}, u32[]{:S(2)}) %copy-start.2) | copy-done | bytes 49176
  3.7 0.0 copy-start.3
  3.7 0.7 %copy-done.3 = f32[5,5]{1,0:T(8,128)S(1)} copy-done((f32[5,5]{1,0:T(8,128)S(1)}, f32[5,5]{1,0:T(8,128)}, u32[]{:S(2)}) %copy-start.3) | copy-done | bytes 124
  4.4 0.0 copy-start.4
  4.4 0.7 %copy-done.4 = s32[8,128]{1,0:T(8,128)S(1)} copy-done((s32[8,128]{1,0:T(8,128)S(1)}, s32[8,128]{1,0:T(8,128)}, u32[]{:S(2)}) %copy-start.4) | copy-done | bytes 4120
  5.1 31.4 %shard_map.64 = f32[5,9,32,128]{3,2,1,0:T(8,128)S(1)} custom-call(f32[5,9,32,128]{3,2,1,0:T(8,128)S(1)} %bitcast.4, f32[5,9,32,128]{3,2,1,0:T(8,128)S(1)} %bitcast.5, f32[3,4,8,128]{3,2,1,0:T(8,128)S(1)} %copy-done.2, f32[5,5]{1,0:T(8,128)S(1)} %copy-done.3, f32[2]{0:T(128)S(1)} %copy-done.5, s32[8,128]{1,0:T(8,128)S(1)} %copy-done.4), custom_call_target="tpu_custom_call" | custom-call | flops 20000000 | bytes 2300000 | tf_op jit(solution)/shard_map/pallas_call | solution.py:361
  36.4 0.9 %copy.8 = f32[5,9,4,8,128]{4,3,2,1,0:T(8,128)} copy(f32[5,9,4,8,128]{4,3,2,1,0:T(8,128)S(1)} %bitcast.3) | data formatting | bytes 1474560
Async XLA Ops:
  0.0 0.7 %copy-start.5 = (f32[2]{0:T(128)S(1)}, f32[2]{0:T(128)}, u32[]{:S(2)}) copy-start(f32[2]{0:T(128)} %rotor_ref.1) | copy-start | bytes 28
  0.7 1.1 %copy-start = (f32[5,9,4,8,128]{4,3,2,1,0:T(8,128)S(1)}, f32[5,9,4,8,128]{4,3,2,1,0:T(8,128)}, u32[]{:S(2)}) copy-start(f32[5,9,4,8,128]{4,3,2,1,0:T(8,128)} %param.6) | copy-start | bytes 2211844
  1.8 1.1 %copy-start.1 = (f32[5,9,4,8,128]{4,3,2,1,0:T(8,128)S(1)}, f32[5,9,4,8,128]{4,3,2,1,0:T(8,128)}, u32[]{:S(2)}) copy-start(f32[5,9,4,8,128]{4,3,2,1,0:T(8,128)} %param.7) | copy-start | bytes 2211844
  2.9 0.8 %copy-start.2 = (f32[3,4,8,128]{3,2,1,0:T(8,128)S(1)}, f32[3,4,8,128]{3,2,1,0:T(8,128)}, u32[]{:S(2)}) copy-start(f32[3,4,8,128]{3,2,1,0:T(8,128)} %velocity_ref.1) | copy-start | bytes 147460
  3.7 0.7 %copy-start.3 = (f32[5,5]{1,0:T(8,128)S(1)}, f32[5,5]{1,0:T(8,128)}, u32[]{:S(2)}) copy-start(f32[5,5]{1,0:T(8,128)} %coupling_ref.1) | copy-start | bytes 304
  4.4 0.7 %copy-start.4 = (s32[8,128]{1,0:T(8,128)S(1)}, s32[8,128]{1,0:T(8,128)}, u32[]{:S(2)}) copy-start(s32[8,128]{1,0:T(8,128)} %map_ref.1) | copy-start | bytes 12292
where the time goes:
time: 37.6 us; the launch traced here: 37.3 us
  Pallas kernels  31.4 us (84%)
  local copies, waits for them, and re-layouts  5.92 us (16%)
    pallas_call x1, Pallas kernels, per_device(): pl.pallas_call(kernel, out_shape=jax.ShapeDtypeStruct(block, f32), in_spe...  31.4 us
    unnamed x13, local copies, waits for them, and re-layouts  5.92 us

commit v1 on v0

v1 whole, which is shorter than its diff:
```python
import functools
import math

import jax
import jax.numpy as jnp
from jax import lax
from jax.experimental import pallas as pl
from jax.experimental.pallas import tpu as pltpu
from jax.sharding import PartitionSpec as P

NVAR = 5
NT = 9
PC = 4
CS = 8
CA = 128
ROWS = PC * CS
CELLS = (PC, CS, CA)
SWEEPS = 3
ROUNDS = SWEEPS + 1
VISCOSITY = 0.1
CFL_RATIO = 3.0
MESH = pl.DeviceIdType.MESH
HALF = (NT - 1) // 2


def cells(rows):
    return rows.reshape(CELLS)


def flat(values):
    return values.reshape(ROWS, CA)


def kernel(
    state_ref, source_ref, velocity_ref, coupling_in, rotor_in, map_in,
    out_ref,
    field, partial, base, forcing, velocity, coef, weight, table, pick,
    beside_sum, shift, inject, mask,
    pitch_ghost, span_send, span_ghost, axial_send, axial_ghost,
    coupling_ref, rotor_ref, map_ref,
    load_sem, send_sem, recv_sem,
):
    place = {a: lax.axis_index(a) for a in ("pitch", "span", "axial")}
    count = {a: lax.axis_size(a) for a in ("pitch", "span", "axial")}
    has = {(a, 0): place[a] > 0 for a in ("span", "axial")}
    has.update({(a, 1): place[a] < count[a] - 1 for a in ("span", "axial")})
    both = {a: jnp.logical_and(has[a, 0], has[a, 1]) for a in ("span", "axial")}
    target = {(a, d): place[a] + 2 * d - 1 for a in ("span", "axial") for d in range(2)}
    target["pitch", 0] = lax.rem(place["pitch"] + count["pitch"] - 1, count["pitch"])
    target["pitch", 1] = lax.rem(place["pitch"] + 1, count["pitch"])
    on_first = place["pitch"] == 0
    on_last = place["pitch"] == count["pitch"] - 1

    def guarded(axis, d, action):
        if axis == "pitch":
            action()
        else:
            pl.when(has[axis, d])(action)

    barrier = pltpu.get_barrier_semaphore()
    for axis in ("pitch", "span", "axial"):
        for d in range(2):

            def greet():
                pl.semaphore_signal(
                    barrier, inc=1, device_id={axis: target[axis, d]}, device_id_type=MESH
                )

            guarded(axis, d, greet)

    loads = [
        pltpu.make_async_copy(src, dst, load_sem.at[n])
        for n, (src, dst) in enumerate(
            (
                (state_ref, field.at[0]),
                (velocity_ref, velocity),
                (source_ref, forcing),
                (coupling_in, coupling_ref),
                (rotor_in, rotor_ref),
                (map_in, map_ref),
            )
        )
    ]
    for load in loads:
        load.start()

    lane = lax.broadcasted_iota(jnp.int32, CELLS, 2)
    row = lax.broadcasted_iota(jnp.int32, (CS, CA), 0)
    lane2 = lax.broadcasted_iota(jnp.int32, (CS, CA), 1)
    row4 = lax.broadcasted_iota(jnp.int32, CELLS, 1)
    slot4 = lax.bitwise_and(lane, 63) - lax.broadcasted_iota(jnp.int32, CELLS, 0)

    def remote(src, dst, k, v, kind, axis, d):
        return pltpu.make_async_remote_copy(
            src_ref=src,
            dst_ref=dst,
            send_sem=send_sem.at[v, kind],
            recv_sem=recv_sem.at[k % 2, v, kind],
            device_id={axis: target[axis, d]},
            device_id_type=MESH,
        )

    def transfers(k, v, kind, axis, d):
        if axis == "pitch":
            faces = state_ref if k == 0 else field.at[k]
            src = faces.at[v, :, pl.ds((ROWS - CS) * d, CS)]
            ghost = pitch_ghost
        elif axis == "span":
            src, ghost = span_send.at[k, d, v], span_ghost
        else:
            src, ghost = axial_send.at[k, v], axial_ghost
        return remote(src, ghost.at[k, 1 - d, v], k, v, kind, axis, d)

    def start(k, v):
        for kind, axis in enumerate(("pitch", "span", "axial")):
            for d in range(2):
                guarded(axis, d, lambda: transfers(k, v, kind, axis, d).start())

    def await_pairs(k, v, arrival):
        for kind, (axis, ghost) in enumerate(
            (("pitch", pitch_ghost), ("span", span_ghost), ("axial", axial_ghost))
        ):

            def one(held, d):
                copy = remote(held, held, k, v, kind, axis, d)
                if arrival:
                    copy.wait_recv()
                else:
                    copy.wait_send()

            if axis == "pitch":
                one(ghost.at[k, :, v], 0)
            else:
                pl.when(both[axis])(lambda: one(ghost.at[k, :, v], 0))
                for d in range(2):
                    alone = jnp.logical_and(has[axis, d], jnp.logical_not(has[axis, 1 - d]))
                    pl.when(alone)(lambda: one(ghost.at[k, d, v], d))

    def pack_span(k, v):
        for i in range(NT):
            at = pl.ds(i * PC, PC)
            span_send[k, 0, v, at, :] = field[k, v, i, pl.ds(0, PC, CS), :]
            span_send[k, 1, v, at, :] = field[k, v, i, pl.ds(CS - 1, PC, CS), :]

    def split(values):
        high = values.astype(jnp.bfloat16)
        low = (values - high.astype(jnp.float32)).astype(jnp.bfloat16)
        return high, low

    def pack_axial(k, v, columns):
        tiles = columns.reshape(NT, PC, CS, CA)
        packed = tiles[0]
        for i in range(1, NT):
            packed = jnp.where(slot4 == i * PC, tiles[i], packed)
        tile = packed[0]
        for p in range(1, PC):
            tile = jnp.where(lax.bitwise_and(lane2, 3) == p, packed[p], tile)
        axial_send[k, v] = tile

    def shifted(k, v, columns):
        values = field[k, v].reshape(NT * ROWS, CA)
        return jnp.dot(
            jnp.concatenate(split(values), axis=1),
            shift[:, columns],
            preferred_element_type=jnp.float32,
        )

    for axis, ghost in (("span", span_ghost), ("axial", axial_ghost)):
        for d in range(2):

            @pl.when(jnp.logical_not(has[axis, d]))
            def _():
                def clear(v, carry):
                    for k in range(ROUNDS):
                        ghost[k, d, v] = jnp.zeros(ghost.shape[3:], jnp.float32)
                    return carry

                lax.fori_loop(0, NVAR, clear, 0)

    source_lane = lax.bitwise_and(lax.broadcasted_iota(jnp.int32, (2 * CA, 2 * CA), 0), CA - 1)
    result_lane = lax.broadcasted_iota(jnp.int32, (2 * CA, 2 * CA), 1)
    adjacent = jnp.abs(source_lane - result_lane) == 1
    spread = source_lane == jnp.where(result_lane < CA + 64, CA - 1, 0)
    shift[...] = jnp.where(
        result_lane < CA, jnp.where(adjacent, 1.0, 0.0), jnp.where(spread, 1.0, 0.0)
    ).astype(jnp.bfloat16)
    source_lane = source_lane[:, :CA]
    result_lane = result_lane[:, :CA]
    inject[...] = jnp.where(
        result_lane == jnp.where(source_lane < 64, 0, CA - 1), 1.0, 0.0
    ).astype(jnp.bfloat16)
    tile_of = lax.broadcasted_iota(jnp.int32, (NT * PC, CS, CA), 0)
    lane_of = lax.broadcasted_iota(jnp.int32, (NT * PC, CS, CA), 2)
    mask[...] = (
        jnp.where(tile_of == lax.bitwise_and(lane_of, 63), 1.0, 0.0)
        .reshape(NT * ROWS, CA)
        .astype(jnp.bfloat16)
        .reshape(NT * PC // 2, 2 * CS, CA)
    )

    loads[0].wait()

    def pack_state(v, carry):
        pack_axial(0, v, shifted(0, v, slice(CA, 2 * CA)))
        pack_span(0, v)
        return carry

    lax.fori_loop(0, NVAR, pack_state, 0)

    waits = 2 + sum(there.astype(jnp.int32) for there in has.values())
    pl.semaphore_wait(barrier, waits)

    def send_state(v, carry):
        start(0, v)
        return carry

    lax.fori_loop(0, NVAR, send_state, 0)

    loads[1].wait()
    radius = [jnp.abs(velocity[d]) + 2.0 * VISCOSITY for d in range(3)]
    scale = CFL_RATIO / (radius[0] + radius[1] + radius[2])
    smoothing = []
    for d in range(3):
        ratio = radius[d] * scale
        smoothing.append(0.25 * jnp.maximum(ratio * ratio - 1.0, 0.0))
    inverse_diagonal = 1.0 / (1.0 + 2.0 * (smoothing[0] + smoothing[1] + smoothing[2]))
    centre = jnp.full(CELLS, -6.0 * VISCOSITY, jnp.float32)
    lower, upper = [], []
    for d in range(3):
        speed = velocity[d]
        lower.append(jnp.maximum(speed, 0.0) + VISCOSITY)
        upper.append(VISCOSITY - jnp.minimum(speed, 0.0))
        centre = centre - jnp.abs(speed)
    smooth = [smoothing[d] * inverse_diagonal for d in range(3)]
    on_top, on_bottom = row4 == CS - 1, row4 == 0
    for held, low, high in ((coef, lower, upper), (weight, smooth, smooth)):
        held[0] = low[0]
        held[1] = high[0]
        held[2] = jnp.where(on_bottom, 0.0, low[1])
        held[3] = jnp.where(on_top, 0.0, high[1])
        held[4] = jnp.where(on_bottom, low[1], 0.0)
        held[5] = jnp.where(on_top, high[1], 0.0)
        held[6] = jnp.where(lane == 0, low[2], high[2])
    weight[7] = inverse_diagonal
    coef[7] = centre
    coef[8] = jnp.where(lane == 0, 0.0, lower[2])
    coef[9] = jnp.where(lane == CA - 1, 0.0, upper[2])

    for load in loads[2:]:
        load.wait()
    rates = [
        rotor_ref[0] * (0.5 * (1 - 2 * (n % 2)) / math.sin(math.pi * n / NT))
        for n in range(1, HALF + 1)
    ]

    zero = jnp.zeros((1, CS, CA), jnp.float32)

    def inside(held, x):
        below = jnp.concatenate([zero, x[: PC - 1]], axis=0)
        above = jnp.concatenate([x[1:], zero], axis=0)
        return (
            held[0] * below
            + held[1] * above
            + held[2] * pltpu.roll(x, 1, 1)
            + held[3] * pltpu.roll(x, CS - 1, 1)
        )

    def local_part(v, carry):
        x = [cells(field[0, v, i]) for i in range(NT)]
        for i in range(NT):
            total = cells(forcing[v, i]) + coef[7] * x[i] + inside(coef, x[i])
            total = total + coef[8] * pltpu.roll(x[i], 1, 2)
            total = total + coef[9] * pltpu.roll(x[i], CA - 1, 2)
            for n in range(1, HALF + 1):
                total = total - rates[n - 1] * (x[(i - n) % NT] - x[(i + n) % NT])
            for w in range(NVAR):
                total = total - coupling_ref[v, w] * cells(field[0, w, i])
            partial[v, i] = flat(total)
        return carry

    lax.fori_loop(0, NVAR, local_part, 0)

    @pl.when(jnp.logical_or(on_first, on_last))
    def _():
        angle = jnp.full((CS, CA), rotor_ref[1], jnp.float32)
        c1 = jnp.cos(angle)
        s1 = jnp.sin(angle) * jnp.where(on_first, 1.0, -1.0)
        c2, s2 = c1 * c1 - s1 * s1, 2.0 * s1 * c1
        c3, s3 = c2 * c1 - s2 * s1, s2 * c1 + c2 * s1
        c4, s4 = c2 * c2 - s2 * s2, 2.0 * s2 * c2
        for n in range(NT):
            total = jnp.full((CS, CA), 1.0 / NT, jnp.float32)
            for h, (c, s) in enumerate(((c1, s1), (c2, s2), (c3, s3), (c4, s4)), 1):
                theta = h * 2.0 * math.pi * n / NT
                total = total + (2.0 / NT * math.cos(theta)) * c - (2.0 / NT * math.sin(theta)) * s
            table[n] = total
        forward = map_ref[...]
        pick[0] = lax.shift_right_logical(forward, 7)
        pick[1] = lax.bitwise_and(forward, CA - 1)

    @pl.when(on_last)
    def _():
        rows, cols = pick[0], pick[1]
        column = lax.broadcasted_iota(jnp.int32, (CA, CA), 0)
        total = jnp.zeros((2 * CS, CA), jnp.float32)
        for s in range(CS):
            hit = rows[s : s + 1, :] == row
            left = jnp.concatenate(
                [
                    jnp.where(hit, float(s), 0.0),
                    jnp.where(hit, lane2.astype(jnp.float32), 0.0),
                ],
                axis=0,
            )
            right = jnp.where(cols[s : s + 1, :] == column, 1.0, 0.0)
            total = total + lax.dot_general(
                left, right, (((1,), (1,)), ((), ())), preferred_element_type=jnp.float32
            )
        pick[0] = total[:CS].astype(jnp.int32)
        pick[1] = total[CS:].astype(jnp.int32)

    def map_face(k, v):
        slot = jnp.where(on_first, 0, 1)

        @pl.when(jnp.logical_or(on_first, on_last))
        def _():
            rows, cols = pick[0], pick[1]
            picked = []
            for i in range(NT):
                total = jnp.zeros((CS, CA), jnp.float32)
                for s in range(CS):
                    line = pitch_ghost[k, slot, v, i, pl.ds(s, 1), :]
                    taken = jnp.take_along_axis(
                        jnp.broadcast_to(line, (CS, CA)), cols, axis=1, mode="promise_in_bounds"
                    )
                    total = jnp.where(rows == s, taken, total)
                picked.append(total)
            for i in range(NT):
                total = table[0] * picked[i]
                for n in range(1, NT):
                    total = total + table[n] * picked[(i - n) % NT]
                pitch_ghost[k, slot, v, i] = total

    def injected(k, v):
        tile = jnp.where(lane2 < 64, axial_ghost[k, 0, v], axial_ghost[k, 1, v])
        left = [
            (part[None] * mask[...]).reshape(NT * ROWS, CA)
            for part in split(jnp.concatenate([tile, tile], axis=0))
        ]
        ends = jnp.dot(
            jnp.concatenate(left, axis=1), inject[...], preferred_element_type=jnp.float32
        )
        return ends.reshape(NT, PC, CS, CA)

    def step(k, v, carry):
        held = coef if k == 0 else weight
        last = k == ROUNDS - 1
        await_pairs(k, v, True)
        map_face(k, v)
        ends = injected(k, v)
        for i in range(NT):
            faces = []
            for p in range(PC):
                at = pl.ds(i * PC + p, 1)
                face = held[4, p] * jnp.broadcast_to(span_ghost[k, 0, v, at, :], (CS, CA))
                face = face + held[5, p] * jnp.broadcast_to(span_ghost[k, 1, v, at, :], (CS, CA))
                if p == 0:
                    face = face + held[0, p] * pitch_ghost[k, 0, v, i]
                if p == PC - 1:
                    face = face + held[1, p] * pitch_ghost[k, 1, v, i]
                faces.append(face)
            total = cells(partial[v, i]) + held[6] * ends[i] + jnp.stack(faces)
            if k == 0:
                base[v, i] = flat(total * weight[7])
            if last:
                out_ref[v, i] = flat(total)
            else:
                field[k + 1, v, i] = flat(total)
        await_pairs(k, v, False)
        if last:
            return carry
        both_sides = shifted(k + 1, v, slice(0, 2 * CA))
        pack_axial(k + 1, v, both_sides[:, CA:])
        pack_span(k + 1, v)
        start(k + 1, v)
        beside_sum[...] = both_sides[:, :CA]
        for i in range(NT):
            x = cells(field[k + 1, v, i])
            around = cells(beside_sum[pl.ds(i * ROWS, ROWS), :])
            total = cells(base[v, i]) + inside(weight, x) + weight[6] * around
            partial[v, i] = flat(total)
        return carry

    for k in range(ROUNDS):
        lax.fori_loop(0, NVAR, functools.partial(step, k), 0)


def per_device(state, source, velocity, coupling, rotor, face_map):
    block = (NVAR, NT, ROWS, CA)
    anywhere = pl.BlockSpec(memory_space=pl.ANY)
    f32 = jnp.float32
    out = pl.pallas_call(
        kernel,
        out_shape=pltpu.VMEM(block, f32),
        in_specs=[anywhere] * 6,
        out_specs=pl.BlockSpec(memory_space=pltpu.VMEM),
        scratch_shapes=[
            pltpu.VMEM((ROUNDS,) + block, f32),
            pltpu.VMEM(block, f32),
            pltpu.VMEM(block, f32),
            pltpu.VMEM(block, f32),
            pltpu.VMEM((3,) + CELLS, f32),
            pltpu.VMEM((10,) + CELLS, f32),
            pltpu.VMEM((8,) + CELLS, f32),
            pltpu.VMEM((NT, CS, CA), f32),
            pltpu.VMEM((2, CS, CA), jnp.int32),
            pltpu.VMEM((NT * ROWS, CA), f32),
            pltpu.VMEM((2 * CA, 2 * CA), jnp.bfloat16),
            pltpu.VMEM((2 * CA, CA), jnp.bfloat16),
            pltpu.VMEM((NT * PC // 2, 2 * CS, CA), jnp.bfloat16),
            pltpu.VMEM((ROUNDS, 2, NVAR, NT, CS, CA), f32),
            pltpu.VMEM((ROUNDS, 2, NVAR, NT * PC, CA), f32),
            pltpu.VMEM((ROUNDS, 2, NVAR, NT * PC, CA), f32),
            pltpu.VMEM((ROUNDS, NVAR, CS, CA), f32),
            pltpu.VMEM((ROUNDS, 2, NVAR, CS, CA), f32),
            pltpu.SMEM((NVAR, NVAR), f32),
            pltpu.SMEM((2,), f32),
            pltpu.VMEM((CS, CA), jnp.int32),
            pltpu.SemaphoreType.DMA((6,)),
            pltpu.SemaphoreType.DMA((NVAR, 3)),
            pltpu.SemaphoreType.DMA((2, NVAR, 3)),
        ],
        compiler_params=pltpu.CompilerParams(
            collective_id=0, has_side_effects=True, vmem_limit_bytes=60 * 1024 * 1024
        ),
        cost_estimate=pl.CostEstimate(flops=20_000_000, bytes_accessed=2_300_000, transcendentals=0),
    )(state.reshape(block), source.reshape(block), velocity, coupling, rotor, face_map)
    return out.reshape(state.shape)


def solution(mesh):
    return jax.shard_map(
        per_device,
        mesh=mesh,
        in_specs=(
            P(None, None, "pitch", "span", "axial"),
            P(None, None, "pitch", "span", "axial"),
            P(None, "pitch", "span", "axial"),
            P(),
            P(),
            P("span", "axial"),
        ),
        out_specs=P(None, None, "pitch", "span", "axial"),
        check_vma=False,
    )
```

time: 37.6 us -> 29.9 us (0.80)
  local copies, waits for them, and re-layouts: 5.92 us -> 0.87 us
  Pallas kernels: 31.4 us -> 28.9 us
    unnamed x13 -> x1, local copies, waits for them, and re-layouts: 5.92 us -> 0.87 us
    pallas_call x1, Pallas kernels: 31.4 us -> 28.9 us  [per_device(): pl.pallas_call(kernel, out_shape=pltpu.VMEM(block, f32), in_specs=[anywhe...]
where the time goes in v1:
time: 29.9 us; the launch traced here: 29.8 us
  Pallas kernels  28.9 us (97%)
  local copies, waits for them, and re-layouts  0.87 us (3%)
    pallas_call x1, Pallas kernels, per_device(): pl.pallas_call(kernel, out_shape=pltpu.VMEM(block, f32), in_specs=[anywhe...  28.9 us
    unnamed x1, local copies, waits for them, and re-layouts  0.87 us

profile of v1, /device:TPU:3, one launch (start us, length us, event | category | flops | bytes accessed | tf_op | source)
XLA Modules:
  0.0 29.8 jit_solution(14621826001744001034)
XLA Ops:
  0.0 28.9 %shard_map.64 = f32[5,9,32,128]{3,2,1,0:T(8,128)S(1)} custom-call(f32[5,9,32,128]{3,2,1,0:T(8,128)} %bitcast.4, f32[5,9,32,128]{3,2,1,0:T(8,128)} %bitcast.5, f32[3,4,8,128]{3,2,1,0:T(8,128)} %velocity_ref.1, f32[5,5]{1,0:T(8,128)} %coupling_in.1, f32[2]{0:T(128)} %rotor_in.1, s32[8,128]{1,0:T(8,128)} %map_in.1), custom_call_target="tpu_custom_call" | custom-call | flops 20000000 | bytes 2300000 | tf_op jit(solution)/shard_map/pallas_call | solution.py:402
  28.9 0.9 %copy.8 = f32[5,9,4,8,128]{4,3,2,1,0:T(8,128)} copy(f32[5,9,4,8,128]{4,3,2,1,0:T(8,128)S(1)} %bitcast.3) | data formatting | bytes 1474560

commit v2 on v1

--- a/solution.py
+++ b/solution.py
@@ -35,17 +35,18 @@
     state_ref, source_ref, velocity_ref, coupling_in, rotor_in, map_in,
     out_ref,
     field, partial, base, forcing, velocity, coef, weight, table, pick,
-    beside_sum, shift, inject, mask,
+    halves, shift, inject, mask,
     pitch_ghost, span_send, span_ghost, axial_send, axial_ghost,
     coupling_ref, rotor_ref, map_ref,
     load_sem, send_sem, recv_sem,
 ):
     place = {a: lax.axis_index(a) for a in ("pitch", "span", "axial")}
     count = {a: lax.axis_size(a) for a in ("pitch", "span", "axial")}
-    has = {(a, 0): place[a] > 0 for a in ("span", "axial")}
-    has.update({(a, 1): place[a] < count[a] - 1 for a in ("span", "axial")})
-    both = {a: jnp.logical_and(has[a, 0], has[a, 1]) for a in ("span", "axial")}
-    target = {(a, d): place[a] + 2 * d - 1 for a in ("span", "axial") for d in range(2)}
+    axes = ("pitch", "span", "axial")
+    has = {(a, 0): place[a] > 0 for a in axes[1:]}
+    has.update({(a, 1): place[a] < count[a] - 1 for a in axes[1:]})
+    both = {a: jnp.logical_and(has[a, 0], has[a, 1]) for a in axes[1:]}
+    target = {(a, d): place[a] + 2 * d - 1 for a in axes[1:] for d in range(2)}
     target["pitch", 0] = lax.rem(place["pitch"] + count["pitch"] - 1, count["pitch"])
     target["pitch", 1] = lax.rem(place["pitch"] + 1, count["pitch"])
     on_first = place["pitch"] == 0
@@ -58,7 +59,7 @@
             pl.when(has[axis, d])(action)
 
     barrier = pltpu.get_barrier_semaphore()
-    for axis in ("pitch", "span", "axial"):
+    for axis in axes:
         for d in range(2):
 
             def greet():
@@ -111,30 +112,28 @@
             src, ghost = axial_send.at[k, v], axial_ghost
         return remote(src, ghost.at[k, 1 - d, v], k, v, kind, axis, d)
 
-    def start(k, v):
-        for kind, axis in enumerate(("pitch", "span", "axial")):
+    def start(k, v, kind):
+        axis = axes[kind]
+        for d in range(2):
+            guarded(axis, d, lambda: transfers(k, v, kind, axis, d).start())
+
+    def await_pair(k, v, kind, arrival):
+        axis, ghost = axes[kind], (pitch_ghost, span_ghost, axial_ghost)[kind]
+
+        def one(held, d):
+            copy = remote(held, held, k, v, kind, axis, d)
+            if arrival:
+                copy.wait_recv()
+            else:
+                copy.wait_send()
+
+        if axis == "pitch":
+            one(ghost.at[k, :, v], 0)
+        else:
+            pl.when(both[axis])(lambda: one(ghost.at[k, :, v], 0))
             for d in range(2):
-                guarded(axis, d, lambda: transfers(k, v, kind, axis, d).start())
-
-    def await_pairs(k, v, arrival):
-        for kind, (axis, ghost) in enumerate(
-            (("pitch", pitch_ghost), ("span", span_ghost), ("axial", axial_ghost))
-        ):
-
-            def one(held, d):
-                copy = remote(held, held, k, v, kind, axis, d)
-                if arrival:
-                    copy.wait_recv()
-                else:
-                    copy.wait_send()
-
-            if axis == "pitch":
-                one(ghost.at[k, :, v], 0)
-            else:
-                pl.when(both[axis])(lambda: one(ghost.at[k, :, v], 0))
-                for d in range(2):
-                    alone = jnp.logical_and(has[axis, d], jnp.logical_not(has[axis, 1 - d]))
-                    pl.when(alone)(lambda: one(ghost.at[k, d, v], d))
+                alone = jnp.logical_not(has[axis, 1 - d])
+                pl.when(alone)(lambda: one(ghost.at[k, d, v], d))
 
     def pack_span(k, v):
         for i in range(NT):
@@ -158,24 +157,17 @@
         axial_send[k, v] = tile
 
     def shifted(k, v, columns):
-        values = field[k, v].reshape(NT * ROWS, CA)
-        return jnp.dot(
-            jnp.concatenate(split(values), axis=1),
-            shift[:, columns],
-            preferred_element_type=jnp.float32,
-        )
-
-    for axis, ghost in (("span", span_ghost), ("axial", axial_ghost)):
-        for d in range(2):
-
-            @pl.when(jnp.logical_not(has[axis, d]))
-            def _():
-                def clear(v, carry):
-                    for k in range(ROUNDS):
-                        ghost[k, d, v] = jnp.zeros(ghost.shape[3:], jnp.float32)
-                    return carry
-
-                lax.fori_loop(0, NVAR, clear, 0)
+        if columns.start:
+            halves[...] = jnp.concatenate(split(field[k, v].reshape(NT * ROWS, CA)), axis=1)
+        return jnp.dot(halves[...], shift[:, columns], preferred_element_type=jnp.float32)
+
+    pl.semaphore_wait(barrier, 2 + sum(there.astype(jnp.int32) for there in has.values()))
+
+    def send_faces(v, carry):
+        start(0, v, 0)
+        return carry
+
+    lax.fori_loop(0, NVAR, send_faces, 0)
 
     source_lane = lax.bitwise_and(lax.broadcasted_iota(jnp.int32, (2 * CA, 2 * CA), 0), CA - 1)
     result_lane = lax.broadcasted_iota(jnp.int32, (2 * CA, 2 * CA), 1)
@@ -202,19 +194,24 @@
 
     def pack_state(v, carry):
         pack_axial(0, v, shifted(0, v, slice(CA, 2 * CA)))
+        start(0, v, 2)
         pack_span(0, v)
+        start(0, v, 1)
         return carry
 
     lax.fori_loop(0, NVAR, pack_state, 0)
 
-    waits = 2 + sum(there.astype(jnp.int32) for there in has.values())
-    pl.semaphore_wait(barrier, waits)
-
-    def send_state(v, carry):
-        start(0, v)
-        return carry
-
-    lax.fori_loop(0, NVAR, send_state, 0)
+    for axis, ghost in (("span", span_ghost), ("axial", axial_ghost)):
+        for d in range(2):
+
+            @pl.when(jnp.logical_not(has[axis, d]))
+            def _():
+                def clear(v, carry):
+                    for k in range(ROUNDS):
+                        ghost[k, d, v] = jnp.zeros(ghost.shape[3:], jnp.float32)
+                    return carry
+
+                lax.fori_loop(0, NVAR, clear, 0)
 
     loads[1].wait()
     radius = [jnp.abs(velocity[d]) + 2.0 * VISCOSITY for d in range(3)]
@@ -242,6 +239,7 @@
         held[5] = jnp.where(on_top, high[1], 0.0)
         held[6] = jnp.where(lane == 0, low[2], high[2])
     weight[7] = inverse_diagonal
+    weight[8] = smooth[2]
     coef[7] = centre
     coef[8] = jnp.where(lane == 0, 0.0, lower[2])
     coef[9] = jnp.where(lane == CA - 1, 0.0, upper[2])
@@ -355,39 +353,49 @@
     def step(k, v, carry):
         held = coef if k == 0 else weight
         last = k == ROUNDS - 1
-        await_pairs(k, v, True)
+
+        def complete(ends, i, p):
+            at = pl.ds(i * PC + p, 1)
+            rows = pl.ds(p * CS, CS)
+            total = partial[v, i, rows] + held[6, p] * ends[i, p]
+            total = total + held[4, p] * jnp.broadcast_to(span_ghost[k, 0, v, at, :], (CS, CA))
+            total = total + held[5, p] * jnp.broadcast_to(span_ghost[k, 1, v, at, :], (CS, CA))
+            if p == 0:
+                total = total + held[0, p] * pitch_ghost[k, 0, v, i]
+            if p == PC - 1:
+                total = total + held[1, p] * pitch_ghost[k, 1, v, i]
+            if k == 0:
+                base[v, i, rows] = total * weight[7, p]
+            if last:
+                out_ref[v, i, rows] = total
+            else:
+                field[k + 1, v, i, rows] = total
+
+        for kind in range(3):
+            await_pair(k, v, kind, False)
+        await_pair(k, v, 0, True)
         map_face(k, v)
+        await_pair(k, v, 2, True)
         ends = injected(k, v)
+        await_pair(k, v, 1, True)
         for i in range(NT):
-            faces = []
-            for p in range(PC):
-                at = pl.ds(i * PC + p, 1)
-                face = held[4, p] * jnp.broadcast_to(span_ghost[k, 0, v, at, :], (CS, CA))
-                face = face + held[5, p] * jnp.broadcast_to(span_ghost[k, 1, v, at, :], (CS, CA))
-                if p == 0:
-                    face = face + held[0, p] * pitch_ghost[k, 0, v, i]
-                if p == PC - 1:
-                    face = face + held[1, p] * pitch_ghost[k, 1, v, i]
-                faces.append(face)
-            total = cells(partial[v, i]) + held[6] * ends[i] + jnp.stack(faces)
-            if k == 0:
-                base[v, i] = flat(total * weight[7])
-            if last:
-                out_ref[v, i] = flat(total)
-            else:
-                field[k + 1, v, i] = flat(total)
-        await_pairs(k, v, False)
+            complete(ends, i, 0)
+            complete(ends, i, PC - 1)
+        if not last:
+            start(k + 1, v, 0)
+        for i in range(NT):
+            for p in range(1, PC - 1):
+                complete(ends, i, p)
         if last:
             return carry
-        both_sides = shifted(k + 1, v, slice(0, 2 * CA))
-        pack_axial(k + 1, v, both_sides[:, CA:])
+        pack_axial(k + 1, v, shifted(k + 1, v, slice(CA, 2 * CA)))
+        start(k + 1, v, 2)
         pack_span(k + 1, v)
-        start(k + 1, v)
-        beside_sum[...] = both_sides[:, :CA]
+        start(k + 1, v, 1)
+        around = shifted(k + 1, v, slice(0, CA)).reshape(NT, PC, CS, CA)
         for i in range(NT):
             x = cells(field[k + 1, v, i])
-            around = cells(beside_sum[pl.ds(i * ROWS, ROWS), :])
-            total = cells(base[v, i]) + inside(weight, x) + weight[6] * around
+            total = cells(base[v, i]) + inside(weight, x) + weight[8] * around[i]
             partial[v, i] = flat(total)
         return carry
 
@@ -411,10 +419,10 @@
             pltpu.VMEM(block, f32),
             pltpu.VMEM((3,) + CELLS, f32),
             pltpu.VMEM((10,) + CELLS, f32),
-            pltpu.VMEM((8,) + CELLS, f32),
+            pltpu.VMEM((9,) + CELLS, f32),
             pltpu.VMEM((NT, CS, CA), f32),
             pltpu.VMEM((2, CS, CA), jnp.int32),
-            pltpu.VMEM((NT * ROWS, CA), f32),
+            pltpu.VMEM((NT * ROWS, 2 * CA), jnp.bfloat16),
             pltpu.VMEM((2 * CA, 2 * CA), jnp.bfloat16),
             pltpu.VMEM((2 * CA, CA), jnp.bfloat16),
             pltpu.VMEM((NT * PC // 2, 2 * CS, CA), jnp.bfloat16),

time: 29.9 us -> 29.7 us (level)
  no operation moved by 1% of the time
where the time goes in v2:
time: 29.7 us; the launch traced here: 29.6 us
  Pallas kernels  28.7 us (97%)
  local copies, waits for them, and re-layouts  0.87 us (3%)
    pallas_call x1, Pallas kernels, per_device(): pl.pallas_call(kernel, out_shape=pltpu.VMEM(block, f32), in_specs=[anywhe...  28.7 us
    unnamed x1, local copies, waits for them, and re-layouts  0.87 us

profile of v2, /device:TPU:3, one launch (start us, length us, event | category | flops | bytes accessed | tf_op | source)
XLA Modules:
  0.0 29.6 jit_solution(10071465562500815862)
XLA Ops:
  0.0 28.7 %shard_map.64 = f32[5,9,32,128]{3,2,1,0:T(8,128)S(1)} custom-call(f32[5,9,32,128]{3,2,1,0:T(8,128)} %bitcast.4, f32[5,9,32,128]{3,2,1,0:T(8,128)} %bitcast.5, f32[3,4,8,128]{3,2,1,0:T(8,128)} %velocity_ref.1, f32[5,5]{1,0:T(8,128)} %coupling_in.1, f32[2]{0:T(128)} %rotor_in.1, s32[8,128]{1,0:T(8,128)} %map_in.1), custom_call_target="tpu_custom_call" | custom-call | flops 20000000 | bytes 2300000 | tf_op jit(solution)/shard_map/pallas_call | solution.py:410
  28.7 0.9 %copy.8 = f32[5,9,4,8,128]{4,3,2,1,0:T(8,128)} copy(f32[5,9,4,8,128]{4,3,2,1,0:T(8,128)S(1)} %bitcast.3) | data formatting | bytes 1474560

commit v3 on v2

--- a/solution.py
+++ b/solution.py
@@ -158,8 +158,8 @@
 
     def shifted(k, v, columns):
         if columns.start:
-            halves[...] = jnp.concatenate(split(field[k, v].reshape(NT * ROWS, CA)), axis=1)
-        return jnp.dot(halves[...], shift[:, columns], preferred_element_type=jnp.float32)
+            halves[v] = jnp.concatenate(split(field[k, v].reshape(NT * ROWS, CA)), axis=1)
+        return jnp.dot(halves[v], shift[:, columns], preferred_element_type=jnp.float32)
 
     pl.semaphore_wait(barrier, 2 + sum(there.astype(jnp.int32) for there in has.values()))
 
@@ -325,13 +325,12 @@
             rows, cols = pick[0], pick[1]
             picked = []
             for i in range(NT):
-                total = jnp.zeros((CS, CA), jnp.float32)
                 for s in range(CS):
                     line = pitch_ghost[k, slot, v, i, pl.ds(s, 1), :]
                     taken = jnp.take_along_axis(
                         jnp.broadcast_to(line, (CS, CA)), cols, axis=1, mode="promise_in_bounds"
                     )
-                    total = jnp.where(rows == s, taken, total)
+                    total = jnp.where(rows == s, taken, total) if s else taken
                 picked.append(total)
             for i in range(NT):
                 total = table[0] * picked[i]
@@ -392,6 +391,9 @@
         start(k + 1, v, 2)
         pack_span(k + 1, v)
         start(k + 1, v, 1)
+        return carry
+
+    def prepare(k, v, carry):
         around = shifted(k + 1, v, slice(0, CA)).reshape(NT, PC, CS, CA)
         for i in range(NT):
             x = cells(field[k + 1, v, i])
@@ -401,6 +403,8 @@
 
     for k in range(ROUNDS):
         lax.fori_loop(0, NVAR, functools.partial(step, k), 0)
+        if k < ROUNDS - 1:
+            lax.fori_loop(0, NVAR, functools.partial(prepare, k), 0)
 
 
 def per_device(state, source, velocity, coupling, rotor, face_map):
@@ -422,7 +426,7 @@
             pltpu.VMEM((9,) + CELLS, f32),
             pltpu.VMEM((NT, CS, CA), f32),
             pltpu.VMEM((2, CS, CA), jnp.int32),
-            pltpu.VMEM((NT * ROWS, 2 * CA), jnp.bfloat16),
+            pltpu.VMEM((NVAR, NT * ROWS, 2 * CA), jnp.bfloat16),
             pltpu.VMEM((2 * CA, 2 * CA), jnp.bfloat16),
             pltpu.VMEM((2 * CA, CA), jnp.bfloat16),
             pltpu.VMEM((NT * PC // 2, 2 * CS, CA), jnp.bfloat16),

time: 29.7 us -> 29.4 us (0.990)
  Pallas kernels: 28.7 us -> 28.4 us
    pallas_call x1, Pallas kernels: 28.7 us -> 28.4 us  [per_device(): pl.pallas_call(kernel, out_shape=pltpu.VMEM(block, f32), in_specs=[anywhe...]
where the time goes in v3:
time: 29.4 us; the launch traced here: 29.3 us
  Pallas kernels  28.4 us (97%)
  local copies, waits for them, and re-layouts  0.87 us (3%)
    pallas_call x1, Pallas kernels, per_device(): pl.pallas_call(kernel, out_shape=pltpu.VMEM(block, f32), in_specs=[anywhe...  28.4 us
    unnamed x1, local copies, waits for them, and re-layouts  0.87 us

profile of v3, /device:TPU:3, one launch (start us, length us, event | category | flops | bytes accessed | tf_op | source)
XLA Modules:
  0.0 29.3 jit_solution(14239872200044444847)
XLA Ops:
  0.0 28.4 %shard_map.64 = f32[5,9,32,128]{3,2,1,0:T(8,128)S(1)} custom-call(f32[5,9,32,128]{3,2,1,0:T(8,128)} %bitcast.4, f32[5,9,32,128]{3,2,1,0:T(8,128)} %bitcast.5, f32[3,4,8,128]{3,2,1,0:T(8,128)} %velocity_ref.1, f32[5,5]{1,0:T(8,128)} %coupling_in.1, f32[2]{0:T(128)} %rotor_in.1, s32[8,128]{1,0:T(8,128)} %map_in.1), custom_call_target="tpu_custom_call" | custom-call | flops 20000000 | bytes 2300000 | tf_op jit(solution)/shard_map/pallas_call | solution.py:414
  28.4 0.9 %copy.8 = f32[5,9,4,8,128]{4,3,2,1,0:T(8,128)} copy(f32[5,9,4,8,128]{4,3,2,1,0:T(8,128)S(1)} %bitcast.3) | data formatting | bytes 1474560

commit v4 on v3

--- a/solution.py
+++ b/solution.py
@@ -353,16 +353,8 @@
         held = coef if k == 0 else weight
         last = k == ROUNDS - 1
 
-        def complete(ends, i, p):
-            at = pl.ds(i * PC + p, 1)
+        def put(i, p, total):
             rows = pl.ds(p * CS, CS)
-            total = partial[v, i, rows] + held[6, p] * ends[i, p]
-            total = total + held[4, p] * jnp.broadcast_to(span_ghost[k, 0, v, at, :], (CS, CA))
-            total = total + held[5, p] * jnp.broadcast_to(span_ghost[k, 1, v, at, :], (CS, CA))
-            if p == 0:
-                total = total + held[0, p] * pitch_ghost[k, 0, v, i]
-            if p == PC - 1:
-                total = total + held[1, p] * pitch_ghost[k, 1, v, i]
             if k == 0:
                 base[v, i, rows] = total * weight[7, p]
             if last:
@@ -372,21 +364,29 @@
 
         for kind in range(3):
             await_pair(k, v, kind, False)
-        await_pair(k, v, 0, True)
-        map_face(k, v)
         await_pair(k, v, 2, True)
         ends = injected(k, v)
         await_pair(k, v, 1, True)
         for i in range(NT):
-            complete(ends, i, 0)
-            complete(ends, i, PC - 1)
-        if not last:
-            start(k + 1, v, 0)
+            for p in range(PC):
+                at = pl.ds(i * PC + p, 1)
+                rows = pl.ds(p * CS, CS)
+                total = partial[v, i, rows] + held[6, p] * ends[i, p]
+                total = total + held[4, p] * jnp.broadcast_to(span_ghost[k, 0, v, at, :], (CS, CA))
+                total = total + held[5, p] * jnp.broadcast_to(span_ghost[k, 1, v, at, :], (CS, CA))
+                if 0 < p < PC - 1:
+                    put(i, p, total)
+                else:
+                    partial[v, i, rows] = total
+        await_pair(k, v, 0, True)
+        map_face(k, v)
         for i in range(NT):
-            for p in range(1, PC - 1):
-                complete(ends, i, p)
+            for d, p in ((0, 0), (1, PC - 1)):
+                face = held[d, p] * pitch_ghost[k, d, v, i]
+                put(i, p, partial[v, i, pl.ds(p * CS, CS)] + face)
         if last:
             return carry
+        start(k + 1, v, 0)
         pack_axial(k + 1, v, shifted(k + 1, v, slice(CA, 2 * CA)))
         start(k + 1, v, 2)
         pack_span(k + 1, v)

time: 29.4 us -> 29.5 us (level)
  no operation moved by 1% of the time
where the time goes in v4:
time: 29.5 us; the launch traced here: 29.4 us
  Pallas kernels  28.5 us (97%)
  local copies, waits for them, and re-layouts  0.87 us (3%)
    pallas_call x1, Pallas kernels, per_device(): pl.pallas_call(kernel, out_shape=pltpu.VMEM(block, f32), in_specs=[anywhe...  28.5 us
    unnamed x1, local copies, waits for them, and re-layouts  0.87 us

profile of v4, /device:TPU:3, one launch (start us, length us, event | category | flops | bytes accessed | tf_op | source)
XLA Modules:
  0.0 29.4 jit_solution(12587593687628120700)
XLA Ops:
  0.0 28.5 %shard_map.64 = f32[5,9,32,128]{3,2,1,0:T(8,128)S(1)} custom-call(f32[5,9,32,128]{3,2,1,0:T(8,128)} %bitcast.4, f32[5,9,32,128]{3,2,1,0:T(8,128)} %bitcast.5, f32[3,4,8,128]{3,2,1,0:T(8,128)} %velocity_ref.1, f32[5,5]{1,0:T(8,128)} %coupling_in.1, f32[2]{0:T(128)} %rotor_in.1, s32[8,128]{1,0:T(8,128)} %map_in.1), custom_call_target="tpu_custom_call" | custom-call | flops 20000000 | bytes 2300000 | tf_op jit(solution)/shard_map/pallas_call | solution.py:414
  28.5 0.9 %copy.8 = f32[5,9,4,8,128]{4,3,2,1,0:T(8,128)} copy(f32[5,9,4,8,128]{4,3,2,1,0:T(8,128)S(1)} %bitcast.3) | data formatting | bytes 1474560
